TPU v7x, 256 devices: a whole 4x4x8 slice. The times are simulated.
256 devices in a mesh: prow: 8 (over y, x_hi), pcol: 32 (over x_lo, z, core).
Axes of the slice: x: 4 (x_hi: 2, x_lo: 2; x = x_hi * 2 + x_lo), y: 4, z: 8, core: 2. Of those that a mesh axis runs over, the one named last changes fastest.
Arguments:
- top_inverse: float32 [24, 512, 24, 512], P(None, ('pcol', 'prow')), as said below
- normed_panel: float32 [2, 4, 512, 6144], P(None, None, 'pcol', 'prow'), may hold values from -0.125 to 0.125
- child_inverse: float32 [2, 6144, 6144], P(None, 'pcol', 'prow'), as said below
- structure: int32 [2, 4], replicated, may hold values from 0 to 23, as said below
Outputs:
- cross_cov: float32 [2, 4, 512, 6144], P(None, None, 'pcol', 'prow')
- child_cov: float32 [2, 6144, 6144], P(None, 'pcol', 'prow')
Inputs may be any that keep to these rules, and one draw needn't show every extreme that they name: top_inverse is symmetric: entry [a, u, b, v] equals entry [b, v, a, u]. child_inverse is symmetric in its last two dimensions. `structure`: each row lists 4 different block numbers in increasing order.
All inputs are finite; a program needn't handle non-finite values.
Results may differ from a plain program's by a relative error of at most 0.0001.
Values sent between devices are 32-bit elements; how exact they have to be, the bound alone decides.
A program may use at most 128 MiB of HBM per device.

v0:
```python
import jax
import jax.numpy as jnp
from jax import lax
from jax.sharding import PartitionSpec as P


def broadcast(value, axis, source):
    kept = jnp.where(lax.axis_index(axis) == source, value, 0).astype(value.dtype)
    return lax.psum(kept, axis)


def select_blocks(top_inverse, structure):
    chosen = []
    for child_index in range(2):
        row_blocks = jnp.take(top_inverse, structure[child_index], axis=0)
        chosen.append(jnp.take(row_blocks, structure[child_index], axis=2))
    return jnp.stack(chosen)


def body(top_inverse, normed_panel, child_inverse, structure):
    picked = select_blocks(top_inverse, structure)
    column_rows = lax.all_gather(picked, "prow", axis=2, tiled=True)
    full_panel = lax.all_gather(normed_panel, "pcol", axis=2, tiled=True)
    cross_cov = -jnp.einsum(
        "caubv,cbvj->cauj", column_rows, full_panel, precision=lax.Precision.HIGHEST
    )
    cross_full = lax.all_gather(cross_cov, "pcol", axis=2, tiled=True)
    width = child_inverse.shape[1]
    col_index = lax.axis_index("pcol")
    groups = lax.axis_size("pcol") // lax.axis_size("prow")
    own_piece = lax.dynamic_slice_in_dim(full_panel, col_index % groups * width, width, 3)
    holder = col_index // groups
    column_panel = broadcast(own_piece, "prow", holder)
    inner_sum = jnp.einsum(
        "cbvj,cbvk->cjk", column_panel, cross_full, precision=lax.Precision.HIGHEST
    )
    child_cov = child_inverse - inner_sum
    return (cross_cov, child_cov)


def solution(mesh):
    in_specs = (
        P(None, ("pcol", "prow"), None, None),
        P(None, None, "pcol", "prow"),
        P(None, "pcol", "prow"),
        P(),
    )
    out_specs = (P(None, None, "pcol", "prow"), P(None, "pcol", "prow"))
    return jax.shard_map(body, mesh=mesh, in_specs=in_specs, out_specs=out_specs, check_vma=False)
```

profile of v0, /device:TPU:1, one launch (start us, length us, event | category | flops | bytes accessed | tf_op | source)
XLA Modules:
  0.0 441.7 jit_solution(3641100337703184921)
XLA Ops:
  7.2 0.0 copy-start
  7.2 0.0 all-gather.6.cloned.1.call-start
  7.2 0.7 all-gather.6.cloned.1.call-update
  7.9 0.0 all-gather.4.cloned.1.call-start
  8.0 0.8 compare_and_fusion.1
  8.7 0.1 copy-done
  8.8 0.6 gather_fusion.2
  9.4 0.6 gather_fusion
  10.0 0.2 broadcast_select_fusion
  10.2 0.3 copy.16
  10.4 0.6 gather_fusion.3
  11.0 0.3 copy.15
  11.3 0.6 gather_fusion.1
  11.9 0.1 select_bitcast_fusion
  12.0 0.1 select_bitcast_fusion.1
  12.1 0.7 copy.17
  12.8 0.0 all-gather.4.cloned.1.call-update
  12.9 0.0 all-reduce.2.cloned.1.call-start
  12.9 81.1 %all-gather.6.cloned.1.call-done = f32[2,4,512,768]{3,2,1,0:T(8,128)} async-done(((f32[2,4,16,768]{3,2,1,0:T(8,128)}), f32[2,4,512,768]{3,2,1,0:T(8,128)}) %all-gather.6.cloned.1.call-update) | async-done | bytes 12582928 | tf_op jit(solution)/shard_map/all_gather | solution.py:23
  94.1 5.9 %dynamic-slice_select_fusion = f32[2,4,512,192]{3,2,1,0:T(8,128)} fusion(f32[2,4,512,768]{3,2,1,0:T(8,128)} %all-gather.6.cloned.1.call-done, s32[]{:T(128)S(6)} %select_n.38, pred[]{:T(512)S(6)} %eq.5), kind=kLoop, calls=%fused_computation.6 | loop fusion | flops 786432 | bytes 6291461 | tf_op jit(solution)/shard_map/jit(_where)/select_n | solution.py:8
  100.0 0.0 all-reduce.2.cloned.1.call-update
  100.0 0.0 copy-start.1
  100.0 0.0 all-gather.8.cloned.1.call-start
  100.1 46.8 %all-gather.4.cloned.1.call-done = f32[2,4,16,4,512]{4,3,1,0,2:T(4,128)} async-done(((f32[2,4,2,4,512]{4,3,1,0,2:T(4,128)}), f32[2,4,16,4,512]{4,3,1,0,2:T(4,128)}) %all-gather.4.cloned.1.call-update) | async-done | bytes 1048592 | tf_op jit(solution)/shard_map/all_gather | solution.py:22
  146.9 12.3 %fusion.6 = f32[2,4,16,768]{3,2,1,0:T(8,128)} fusion(f32[2,4,512,768]{3,2,1,0:T(8,128)} %all-gather.6.cloned.1.call-done, f32[2,4,16,4,512]{4,3,1,0,2:T(4,128)} %all-gather.4.cloned.1.call-done), kind=kOutput, calls=%fused_computation.10 | convolution fusion | flops 2416017408 | bytes 14024704 | tf_op jit(solution)/shard_map/caubv,cbvj->cauj/dot_general | solution.py:24
  159.2 0.0 all-gather.8.cloned.1.call-update
  159.2 180.4 %all-reduce.2.cloned.1.call-done = f32[2,4,512,192]{3,2,1,0:T(8,128)} async-done(((f32[2,4,512,192]{3,2,1,0:T(8,128)}), f32[2,4,512,192]{3,2,1,0:T(8,128)}) %all-reduce.2.cloned.1.call-update) | async-done | bytes 3145744 | tf_op jit(solution)/shard_map/psum | solution.py:9
  339.6 82.0 %all-gather.8.cloned.1.call-done = f32[2,4,512,768]{3,2,1,0:T(8,128)} async-done(((f32[2,4,16,768]{3,2,1,0:T(8,128)}), f32[2,4,512,768]{3,2,1,0:T(8,128)}) %all-gather.8.cloned.1.call-update) | async-done | bytes 12582928 | tf_op jit(solution)/shard_map/all_gather | solution.py:27
  421.7 0.0 copy-done.1
  421.7 13.5 %fusion.2 = f32[2,192,768]{2,1,0:T(8,128)} fusion(f32[2,192,768]{2,1,0:T(8,128)S(1)} %copy-done.1, f32[2,4,512,192]{3,2,1,0:T(8,128)} %all-reduce.2.cloned.1.call-done, f32[2,4,512,768]{3,2,1,0:T(8,128)} %all-gather.8.cloned.1.call-done), kind=kOutput, calls=%fused_computation.8 | convolution fusion | flops 7248052224 | bytes 18087936 | tf_op jit(solution)/shard_map/cbvj,cbvk->cjk/dot_general | solution.py:34
  (3 shorter events, 0.0 us)
Async XLA Ops:
  7.2 1.7 copy-start
  7.2 86.9 %all-gather.6.cloned.1.call-start = ((), (), s32[]{:S(2)}) async-start(), calls=%async_computation.1 | async-start | bytes 12976128 | tf_op jit(solution)/shard_map/all_gather | solution.py:23
  7.9 139.0 %all-gather.4.cloned.1.call-start = ((), (), s32[]{:S(2)}) async-start(), calls=%async_computation | async-start | bytes 1179648 | tf_op jit(solution)/shard_map/all_gather | solution.py:22
  12.9 326.8 %all-reduce.2.cloned.1.call-start = ((), (), s32[]{:S(2)}) async-start(), calls=%async_computation.2 | async-start | bytes 8388608 | tf_op jit(solution)/shard_map/psum | solution.py:9
  100.0 321.7 %copy-start.1 = (f32[2,192,768]{2,1,0:T(8,128)S(1)}, f32[2,192,768]{2,1,0:T(8,128)}, u32[]{:S(2)}) copy-start(f32[2,192,768]{2,1,0:T(8,128)} %param.10) | copy-start | bytes 3538948
  100.0 321.7 %all-gather.8.cloned.1.call-start = ((), (), s32[]{:S(2)}) async-start(), calls=%async_computation.3 | async-start | bytes 12976128 | tf_op jit(solution)/shard_map/all_gather | solution.py:27
Sparse Core Ops, SparseCore 0:
  9.8 84.2 all-gather.5
  97.3 49.5 all-gather.3
  149.6 190.0 all-reduce.1
  341.9 79.7 all-gather.7
where the time goes:
time: 442 us
  waiting for transfers between devices  391 us (88%)
  matrix products  25.8 us (6%)
  between operations  13.9 us (3%)
  other arithmetic  7 us (2%)
    psum x1, waiting for transfers between devices, broadcast(): return lax.psum(kept, axis)  180 us
    all_gather x1, waiting for transfers between devices, body(): cross_full = lax.all_gather(cross_cov, 'pcol', axis=2, tiled=True)  82 us
    all_gather x1, waiting for transfers between devices, body(): full_panel = lax.all_gather(normed_panel, 'pcol', axis=2, tiled=True)  81.1 us
    all_gather x1, waiting for transfers between devices, body(): column_rows = lax.all_gather(picked, 'prow', axis=2, tiled=True)  46.8 us
    dot_general x1, matrix products, body(): jnp.einsum('cbvj,cbvk->cjk', column_panel, cross_full, precision=lax.Prec...  13.5 us
    dot_general x1, matrix products, body(): jnp.einsum('caubv,cbvj->cauj', column_rows, full_panel, precision=lax.Pre...  12.3 us
  transfers between devices with their start and end apart: 4, of which 4 were waited for; matrix products, arithmetic and copies ran while one was open for 5% of the time, Pallas kernels for 0%

commit v1 on v0

v1 whole, which is shorter than its diff:
```python
import jax
import jax.numpy as jnp
from jax import lax
from jax.experimental import pallas as pl
from jax.experimental.pallas import tpu as pltpu
from jax.sharding import PartitionSpec as P

MESH = pl.DeviceIdType.MESH
F32, BF16 = jnp.float32, jnp.bfloat16
NCHUNK = 3
QUAD = ((0, 1), (1, 0), (1, 1))
PLANE = 8


def bit_xor(a, b):
    return lax.rem(a + b, 2)


def split(x):
    hi = x.astype(BF16)
    return hi, (x - hi.astype(F32)).astype(BF16)


def mm(a, b):
    return jnp.dot(a, b, preferred_element_type=F32)


def mm3(a_hi, a_lo, b_hi, b_lo):
    return mm(a_hi, b_hi) + (mm(a_hi, b_lo) + mm(a_lo, b_hi))


def kernel(structure, top, panel, inverse, cross, cov, sel, s_all, s_hi, s_lo, p_all, p_hi, p_lo,
           x_own, x_send, x_mid, x_all, g_own, g_in, c_in, ss, rs):
    row, col = lax.axis_index("prow"), lax.axis_index("pcol")
    child, z, core = lax.div(col, 16), lax.rem(lax.div(col, 2), 8), lax.rem(col, 2)

    def at(r, c, zz, j):
        return (r, (c * 8 + lax.rem(zz + 8, 8)) * 2 + j)

    def quad(d):
        return bit_xor(child, d[0]), bit_xor(core, d[1])

    counter = [0]

    def sems(count):
        base = counter[0]
        counter[0] += count
        return base

    pending = []

    def send(src, dst, index, device, own=None):
        out = index if own is None else own
        copy = pltpu.make_async_remote_copy(src, dst, ss.at[out], rs.at[index], device_id=device, device_id_type=MESH)
        copy.start()
        return copy

    def wait_recv(landing, index):
        pltpu.make_async_remote_copy(landing, landing, ss.at[index], rs.at[index], device_id=(row, col), device_id_type=MESH).wait_recv()

    sib = at(row, child, z, 1 - core)
    half, quarter = lax.div(row, 4), lax.rem(row, 4)
    m, s = lax.div(z, 2), lax.rem(z, 2)
    sw = bit_xor(half, s)
    e = lax.rem(quarter - m - 2 * half + 8, 4)
    mid_row = 4 * sw + 2 * lax.div(e, 2) + bit_xor(lax.rem(e, 2), sw)
    mid_self = mid_row == row
    sw2 = lax.div(row, 4)
    e2 = 2 * lax.div(quarter, 2) + bit_xor(lax.rem(quarter, 2), sw2)
    half2 = bit_xor(sw2, s)
    q2 = lax.rem(e2 + m + 2 * half2, 4)
    far_z = 2 * q2 + core
    far = at(row, child, far_z, half2)
    far_self = (far_z == z) & (half2 == core)
    half3 = core
    m3 = lax.rem(m - e2 - 2 * half3 + 8, 4)
    s3 = bit_xor(sw2, half3)
    from_z = 2 * m3 + s3
    from_core = s
    src_far = at(row, child, from_z, from_core)

    def piece_z(r, h):
        w = lax.div(r, 4)
        k = lax.rem(r, 4)
        ee = 2 * lax.div(k, 2) + bit_xor(lax.rem(k, 2), w)
        return 2 * lax.rem(m - ee - 2 * h + 8, 4) + bit_xor(w, h)

    barrier = pltpu.get_barrier_semaphore()

    def greet(device):
        pl.semaphore_signal(barrier, inc=1, device_id=device, device_id_type=MESH)

    for d in QUAD:
        greet(at(row, quad(d)[0], z, quad(d)[1]))
    greet(at(row, child, z + 1, core))
    greet(at(row, child, z - 1, core))
    for d in range(1, PLANE):
        greet((lax.rem(row + d, PLANE), col))

    @pl.when(jnp.logical_not(far_self))
    def _():
        greet(far)
        greet(src_far)

    for c in range(2):
        for a in range(4):
            for u in range(2):
                for b in range(4):
                    sel[c, 2 * a + u:2 * a + u + 1, 512 * b:512 * b + 512] = top[structure[c, a], u, pl.ds(structure[c, b], 1), :]

    pl.semaphore_wait(barrier, 12 + 2 * (1 - far_self.astype(jnp.int32)))

    i_quad = sems(3 * NCHUNK)

    def quad_send(n):
        for k, d in enumerate(QUAD):
            c2, j2 = quad(d)
            cols = pl.ds(pl.multiple_of(384 * j2 + 128 * n, 128), 128)
            pending.append(send(panel.at[c2, :, :, :, cols], p_all.at[n, :, z, :, child, pl.ds(pl.multiple_of(16 * core, 16), 16), :],
                                i_quad + 3 * n + k, at(row, c2, z, j2)))
        cols = pl.ds(pl.multiple_of(384 * core + 128 * n, 128), 128)
        p_all[n, :, z, :, child, pl.ds(pl.multiple_of(16 * core, 16), 16), :] = panel[child, :, :, :, cols]

    def quad_wait(n):
        for k, d in enumerate(QUAD):
            c2, j2 = quad(d)
            wait_recv(p_all.at[n, :, z, :, c2, pl.ds(pl.multiple_of(16 * j2, 16), 16), :], i_quad + 3 * n + k)

    i_sx = sems(1)
    mine = 2 * row + core
    quad_send(0)
    pending.append(send(sel.at[1 - child], s_all.at[mine, child], i_sx, at(row, 1 - child, z, core)))
    s_all[mine, child] = sel[child]
    quad_send(1)
    quad_send(2)

    i_right, i_left = sems(8 * NCHUNK), sems(8 * NCHUNK)

    def chunk(n, h, zz):
        return p_all.at[n, h, lax.rem(zz + 16, 8)]

    def right_wait(n, h, step):
        wait_recv(chunk(n, h, z - 1 - step), i_right + 8 * n + 4 * h + step)

    def left_wait(n, h, step):
        wait_recv(chunk(n, h, z + 1 + step), i_left + 8 * n + 4 * h + step)

    def ring(n, step):
        for h in range(2):
            if step < 3 or h == 0:
                if step:
                    right_wait(n, h, step - 1)
                piece = chunk(n, h, z - step)
                pending.append(send(piece, piece, i_right + 8 * n + 4 * h + step, at(row, child, z + 1, core)))
            if step < 3 or h == 1:
                if step:
                    left_wait(n, h, step - 1)
                piece = chunk(n, h, z + step)
                pending.append(send(piece, piece, i_left + 8 * n + 4 * h + step, at(row, child, z - 1, core)))

    def ring_end(n):
        right_wait(n, 1, 2)
        left_wait(n, 0, 2)
        right_wait(n, 0, 3)
        left_wait(n, 1, 3)
        for h in range(2):
            for zz in range(8):
                hi, lo = split(p_all[n, h, zz])
                p_hi[2 * h:2 * h + 2, :, zz, :, 128 * n:128 * n + 128] = hi
                p_lo[2 * h:2 * h + 2, :, zz, :, 128 * n:128 * n + 128] = lo

    def plane_send(buf, base):
        for d in range(1, PLANE):
            pending.append(send(buf.at[mine], buf.at[mine], base + d, (lax.rem(row + d, PLANE), col)))
        pending.append(send(buf.at[mine], buf.at[mine], base + 8, sib))

    def plane_pass(buf, base):
        for d in range(1, PLANE):
            slot = 2 * lax.rem(row - d + PLANE, PLANE) + core
            wait_recv(buf.at[slot], base + d)
            pending.append(send(buf.at[slot], buf.at[slot], base + 8 + d, sib))

    def plane_end(buf, base):
        for d in range(PLANE):
            wait_recv(buf.at[2 * lax.rem(row - d + PLANE, PLANE) + 1 - core], base + 8 + d)

    i_s = sems(16)
    i_x = [sems(16) for _ in range(NCHUNK)]
    i_mid, i_far = sems(NCHUNK), sems(NCHUNK)
    i_cross = sems(3 * NCHUNK)
    i_g, i_gs = sems(12), sems(6)

    def s_end():
        plane_pass(s_all, i_s)
        plane_end(s_all, i_s)
        pos = lax.broadcasted_iota(jnp.int32, (256, 256), 0)
        old = lax.broadcasted_iota(jnp.int32, (256, 256), 1)
        a, k, j, r, u = pos >> 6, (pos >> 5) & 1, (pos >> 4) & 1, (pos >> 1) & 7, pos & 1
        order = jnp.where(old == r * 32 + j * 16 + k * 8 + a * 2 + u, 1.0, 0.0).astype(BF16)
        hi, lo = split(s_all[...].reshape(256, 2048))
        s_hi[...] = mm(order, hi).astype(BF16)
        s_lo[...] = mm(order, lo).astype(BF16)

    def x_compute(n):
        cols = slice(128 * n, 128 * n + 128)
        b_hi = p_hi[:, :, :, :, cols].reshape(2048, 128)
        b_lo = p_lo[:, :, :, :, cols].reshape(2048, 128)
        x = -mm3(s_hi[...], s_lo[...], b_hi, b_lo)
        x_own[n] = x.reshape(4, 2, 32, 128)
        x_send[n] = x.T

        @pl.when(mid_self)
        def _():
            x_mid[n] = x_send[n]

        @pl.when(jnp.logical_not(mid_self))
        def _():
            send(x_send.at[n], x_mid.at[n], i_mid + n, (mid_row, col))

    def cross_send(n):
        for k, d in enumerate(QUAD):
            c2, j2 = quad(d)
            pending.append(send(x_own.at[n, :, c2, pl.ds(pl.multiple_of(16 * j2, 16), 16), :], c_in.at[child, core, n],
                                i_cross + 3 * n + k, at(row, c2, z, j2)))
        c_in[child, core, n] = x_own[n, :, child, pl.ds(pl.multiple_of(16 * core, 16), 16), :]

    def cross_end(n):
        for k, d in enumerate(QUAD):
            c2, j2 = quad(d)
            wait_recv(c_in.at[c2, j2, n], i_cross + 3 * n + k)

    def mid_pass(n):
        slot = 2 * row + half2

        @pl.when(jnp.logical_not(mid_self))
        def _():
            wait_recv(x_mid.at[n], i_mid + n)

        @pl.when(far_self)
        def _():
            x_all[n, mine] = x_mid[n]

        @pl.when(jnp.logical_not(far_self))
        def _():
            send(x_mid.at[n], x_all.at[n, slot], i_far + n, far)

    def far_pass(n):
        @pl.when(jnp.logical_not(far_self))
        def _():
            wait_recv(x_all.at[n, mine], i_far + n)
        plane_send(x_all.at[n], i_x[n])

    def g_compute(n):
        plane_pass(x_all.at[n], i_x[n])
        plane_end(x_all.at[n], i_x[n])
        for rel in range(2):
            h = bit_xor(child, rel)

            def step(r, acc):
                zz = piece_z(r, h)
                x_hi, x_lo = split(x_all[n, 2 * r + h])
                b_hi = p_hi[:, :, zz].reshape(256, 384)
                b_lo = p_lo[:, :, zz].reshape(256, 384)
                return acc + mm3(x_hi, x_lo, b_hi, b_lo)

            g_own[n, rel] = lax.fori_loop(0, PLANE, step, jnp.zeros((128, 384), F32))

    def unit(n, rel, i):
        return g_own.at[n, rel, pl.ds(64 * i, 64), :]

    def g_send(n):
        for i in range(2):
            t = 2 * n + i
            j2, k = t // 3, t % 3
            pending.append(send(unit(n, 1, i), g_in.at[child, core, k], i_g + 6 + 3 * core + k, at(row, 1 - child, z, j2), i_gs + t))

            @pl.when(core == j2)
            def _():
                g_in[child, core, k] = g_own[n, 0, 64 * i:64 * i + 64]

            @pl.when(core != j2)
            def _():
                send(unit(n, 0, i), g_in.at[child, core, k], i_g + 3 * core + k, sib)

    def g_end():
        for k in range(3):
            wait_recv(g_in.at[child, 1 - core, k], i_g + 3 * (1 - core) + k)
            for h in range(2):
                wait_recv(g_in.at[1 - child, h, k], i_g + 6 + 3 * h + k)

    quad_wait(0)
    ring(0, 0)
    wait_recv(s_all.at[mine, 1 - child], i_sx)
    plane_send(s_all, i_s)
    ring(0, 1)
    quad_wait(1)
    quad_wait(2)
    ring(0, 2)
    ring(0, 3)
    ring(1, 0)
    s_end()
    ring_end(0)
    x_compute(0)
    ring(1, 1)
    cross_send(0)
    mid_pass(0)
    ring(1, 2)
    far_pass(0)
    ring(1, 3)
    ring(2, 0)
    ring_end(1)
    x_compute(1)
    ring(2, 1)
    cross_send(1)
    mid_pass(1)
    ring(2, 2)
    far_pass(1)
    ring(2, 3)
    ring_end(2)
    x_compute(2)
    cross_send(2)
    mid_pass(2)
    g_compute(0)
    g_send(0)
    far_pass(2)
    g_compute(1)
    g_send(1)
    for n in range(NCHUNK):
        cross_end(n)
    for c in range(2):
        for h in range(2):
            for n in range(NCHUNK):
                cross[c, :, :, 384 * h + 128 * n:384 * h + 128 * n + 128] = c_in[c, h, n]
    g_compute(2)
    g_send(2)
    g_end()
    for c in range(2):
        for h in range(2):
            cov[c, :, 384 * h:384 * h + 384] = inverse[c, :, 384 * h:384 * h + 384] - g_in[c, h].reshape(192, 384)

    for copy in pending:
        copy.wait_send()

    def late(src, dst, index):
        pltpu.make_async_remote_copy(src, dst, ss.at[index], rs.at[index], device_id=(row, col), device_id_type=MESH).wait_send()

    for n in range(NCHUNK):
        @pl.when(jnp.logical_not(mid_self))
        def _():
            late(x_send.at[n], x_mid.at[n], i_mid + n)

        @pl.when(jnp.logical_not(far_self))
        def _():
            late(x_mid.at[n], x_all.at[n, mine], i_far + n)

        for i in range(2):
            t = 2 * n + i

            @pl.when(core != t // 3)
            def _():
                late(unit(n, 0, i), g_in.at[child, core, t % 3], i_g + 3 * core + t % 3)


N_SEMS = 9 + 1 + 48 + 16 + 48 + 6 + 9 + 12 + 6


def body(top_inverse, normed_panel, child_inverse, structure):
    vmem = pl.BlockSpec(memory_space=pltpu.VMEM)
    panel = normed_panel.reshape(2, 2, 2, 16, 768)
    return pl.pallas_call(
        kernel,
        out_shape=(jax.ShapeDtypeStruct((2, 4, 16, 768), F32), jax.ShapeDtypeStruct((2, 192, 768), F32)),
        in_specs=[pl.BlockSpec(memory_space=pltpu.SMEM), vmem, vmem, vmem],
        out_specs=(vmem, vmem),
        scratch_shapes=[
            pltpu.VMEM((2, 8, 2048), F32),
            pltpu.VMEM((16, 2, 8, 2048), F32),
            pltpu.VMEM((256, 2048), BF16),
            pltpu.VMEM((256, 2048), BF16),
            pltpu.VMEM((NCHUNK, 2, 8, 2, 2, 32, 128), F32),
            pltpu.VMEM((4, 2, 8, 32, 384), BF16),
            pltpu.VMEM((4, 2, 8, 32, 384), BF16),
            pltpu.VMEM((NCHUNK, 4, 2, 32, 128), F32),
            pltpu.VMEM((NCHUNK, 128, 256), F32),
            pltpu.VMEM((NCHUNK, 128, 256), F32),
            pltpu.VMEM((NCHUNK, 16, 128, 256), F32),
            pltpu.VMEM((NCHUNK, 2, 128, 384), F32),
            pltpu.VMEM((2, 2, 3, 64, 384), F32),
            pltpu.VMEM((2, 2, NCHUNK, 4, 16, 128), F32),
            pltpu.SemaphoreType.DMA((N_SEMS,)),
            pltpu.SemaphoreType.DMA((N_SEMS,)),
        ],
        compiler_params=pltpu.CompilerParams(collective_id=0, has_side_effects=True, vmem_limit_bytes=48 * 2**20),
        name="selected_inverse",
    )(structure, top_inverse, panel, child_inverse)


def solution(mesh):
    in_specs = (
        P(None, ("pcol", "prow"), None, None),
        P(None, None, "pcol", "prow"),
        P(None, "pcol", "prow"),
        P(),
    )
    out_specs = (P(None, None, "pcol", "prow"), P(None, "pcol", "prow"))
    return jax.shard_map(body, mesh=mesh, in_specs=in_specs, out_specs=out_specs, check_vma=False)
```

time: 442 us -> 130 us (0.29)
  the two profiles are of different devices: /device:TPU:1 before, /device:TPU:19 now
where the time goes in v1:
time: 130 us; the launch traced here: 129 us
  Pallas kernels  122 us (94%)
  local copies, waits for them, and re-layouts  6.36 us (5%)
    pallas_call x1, Pallas kernels, body(): pl.pallas_call(kernel, out_shape=(jax.ShapeDtypeStruct((2, 4, 16, 768), F...  122 us
    unnamed x10, local copies, waits for them, and re-layouts  6.36 us

profile of v1, /device:TPU:19, one launch (start us, length us, event | category | flops | bytes accessed | tf_op | source)
XLA Modules:
  0.0 129.5 jit_solution(10713723098545408418)
XLA Ops:
  0.6 0.0 copy-start
  0.6 1.7 %copy-done = f32[24,2,24,512]{3,2,1,0:T(8,128)S(1)} copy-done((f32[24,2,24,512]{3,2,1,0:T(8,128)S(1)}, f32[24,2,24,512]{3,2,1,0:T(8,128)}, u32[]{:S(2)}) %copy-start) | copy-done | bytes 2359320
  2.3 0.0 copy-start.1
  2.3 1.3 copy-done.1
  3.6 0.0 copy-start.2
  3.6 1.0 copy-done.2
  4.6 0.0 copy-start.3
  4.6 0.7 copy-done.3
  5.2 122.4 %selected_inverse.1 = (f32[2,4,16,768]{3,2,1,0:T(8,128)S(1)}, f32[2,192,768]{2,1,0:T(8,128)S(1)}) custom-call(s32[2,4]{1,0:T(2,128)S(1)} %copy-done.3, f32[24,2,24,512]{3,2,1,0:T(8,128)S(1)} %copy-done, f32[2,2,2,16,768]{4,3,2,1,0:T(8,128)S(1)} %bitcast.1, f32[2,192,768]{2,1,0:T(8,128)S(1)} %copy-done.1), custom_call_target="tpu_custom_call" | custom-call | tf_op jit(solution)/shard_map/selected_inverse/pallas_call | solution.py:370
  127.7 0.7 copy.8
  128.4 1.0 copy.9
Async XLA Ops:
  0.6 1.7 %copy-start = (f32[24,2,24,512]{3,2,1,0:T(8,128)S(1)}, f32[24,2,24,512]{3,2,1,0:T(8,128)}, u32[]{:S(2)}) copy-start(f32[24,2,24,512]{3,2,1,0:T(8,128)} %top.1) | copy-start | bytes 7077892
  2.3 1.3 copy-start.1
  3.6 1.0 copy-start.2
  4.6 0.7 copy-start.3

commit v2 on v0

v2 whole, which is shorter than its diff:
```python
import functools

import jax
import jax.numpy as jnp
from jax import lax
from jax.experimental import pallas as pl
from jax.experimental.pallas import tpu as pltpu
from jax.sharding import PartitionSpec as P

MESH = pl.DeviceIdType.MESH
F32, BF16 = jnp.float32, jnp.bfloat16
NCHUNK = 6
QUAD = ((0, 1), (1, 0), (1, 1))
PLANE = 8


def bit_xor(a, b):
    return lax.rem(a + b, 2)


def split(x):
    hi = x.astype(BF16)
    return hi, (x - hi.astype(F32)).astype(BF16)


def merge(a, b):
    lane = lax.broadcasted_iota(jnp.int32, a.shape, a.ndim - 1)
    return jnp.where(lane < 64, a, pltpu.roll(b, 64, a.ndim - 1))


def merge_high(a, b):
    lane = lax.broadcasted_iota(jnp.int32, a.shape, a.ndim - 1)
    return jnp.where(lane < 64, pltpu.roll(a, 64, a.ndim - 1), b)


def mm(a, b):
    return jnp.dot(a, b, preferred_element_type=F32)


def kernel(structure, top_hbm, panel_hbm, inverse_hbm, cross, cov, top, panel, packed, inverse, sel, s_all, s_cat, p_all, k_hi, k_lo, p_hi, p_lo,
           x_own, x_send, x_mid, x_all, x_cat, g_own, g_in, c_in, ss, rs, ls):
    row, col = lax.axis_index("prow"), lax.axis_index("pcol")
    child, z, core = lax.div(col, 16), lax.rem(lax.div(col, 2), 8), lax.rem(col, 2)

    def at(r, c, zz, j):
        return (r, (c * 8 + lax.rem(zz + 8, 8)) * 2 + j)

    def quad(d):
        return bit_xor(child, d[0]), bit_xor(core, d[1])

    counts = [0, 0]

    def sems(side, count=1):
        counts[side] += count
        return counts[side] - count

    def send(src, dst, out, into, device):
        pltpu.make_async_remote_copy(src, dst, ss.at[out], rs.at[into], device_id=device, device_id_type=MESH).start()

    def wait_send(ref, index):
        pltpu.make_async_remote_copy(ref, ref, ss.at[index], rs.at[0], device_id=(row, col), device_id_type=MESH).wait_send()

    def wait_recv(ref, index):
        pltpu.make_async_remote_copy(ref, ref, ss.at[0], rs.at[index], device_id=(row, col), device_id_type=MESH).wait_recv()

    sib = at(row, child, z, 1 - core)
    half, quarter = lax.div(row, 4), lax.rem(row, 4)
    m, s = lax.div(z, 2), lax.rem(z, 2)
    sw = bit_xor(half, s)
    e = lax.rem(quarter - m - 2 * half + 8, 4)
    mid_row = 4 * sw + 2 * lax.div(e, 2) + bit_xor(lax.rem(e, 2), sw)
    mid_self = mid_row == row
    sw2 = lax.div(row, 4)
    e2 = 2 * lax.div(quarter, 2) + bit_xor(lax.rem(quarter, 2), sw2)
    half2 = bit_xor(sw2, s)
    q2 = lax.rem(e2 + m + 2 * half2, 4)
    far_z = 2 * q2 + core
    far = at(row, child, far_z, half2)
    far_self = (far_z == z) & (half2 == core)
    half3 = core
    m3 = lax.rem(m - e2 - 2 * half3 + 8, 4)
    s3 = bit_xor(sw2, half3)
    from_z = 2 * m3 + s3
    from_core = s
    src_far = at(row, child, from_z, from_core)

    loads = [pltpu.make_async_copy(a, b, ls.at[i]) for i, (a, b) in enumerate(((panel_hbm, panel), (top_hbm, top), (inverse_hbm, inverse)))]
    for load in loads:
        load.start()
    barrier = pltpu.get_barrier_semaphore()

    def greet(device):
        pl.semaphore_signal(barrier, inc=1, device_id=device, device_id_type=MESH)

    for d in QUAD:
        greet(at(row, quad(d)[0], z, quad(d)[1]))
    greet(at(row, child, z + 1, core))
    greet(at(row, child, z - 1, core))
    for d in range(1, PLANE):
        greet((lax.rem(row + d, PLANE), col))
        greet(at(lax.rem(row + d, PLANE), 1 - child, z, core))

    @pl.when(jnp.logical_not(far_self))
    def _():
        greet(far)
        greet(src_far)

    loads[0].wait()
    for c in range(2):
        for j in range(2):
            for n in range(3):
                for b in range(2):
                    low = panel[c, 0, b, :, 384 * j + 128 * n:384 * j + 128 * n + 128]
                    high = panel[c, 1, b, :, 384 * j + 128 * n:384 * j + 128 * n + 128]
                    packed[c, j, 2 * n, b] = merge(low, high)
                    packed[c, j, 2 * n + 1, b] = merge_high(low, high)
    for t in range(NCHUNK):
        p_all[t, z, :, child, pl.ds(pl.multiple_of(16 * core, 16), 16), :] = packed[child, core, t]
    pl.semaphore_wait(barrier, 19 + 2 * (1 - far_self.astype(jnp.int32)))

    out_quad, in_quad = sems(0, 3), sems(1, 3)

    def quad_send(n):
        for k, d in enumerate(QUAD):
            c2, j2 = quad(d)
            send(packed.at[c2, j2, 2 * n:2 * n + 2], p_all.at[2 * n:2 * n + 2, z, :, child, pl.ds(pl.multiple_of(16 * core, 16), 16), :],
                 out_quad + k, in_quad + n, at(row, c2, z, j2))

    def quad_wait(n):
        wait_recv(packed.at[0, 0], in_quad + n)

    def select():
        loads[1].wait()
        for c in range(2):
            for a in range(4):
                for u in range(2):
                    for b in range(4):
                        sel[c, 2 * a + u:2 * a + u + 1, 512 * b:512 * b + 512] = top[structure[c, a], u, pl.ds(structure[c, b], 1), :]
        s_all[row, core, child] = sel[child]

    out_ring, in_ring = sems(0), sems(1, 4 * NCHUNK)

    def chunk(n, zz, part=None):
        ref = p_all.at[n, lax.rem(zz + 16, 8)]
        return ref if part is None else ref.at[part]

    def ring_wait(n, step):
        wait_recv(p_all.at[n, 0:2 if step < 3 else 1], in_ring + 4 * n + step)

    def ring(n, step):
        if step:
            ring_wait(n, step - 1)
        for side, part in ((1, 0), (-1, 1)):
            block = chunk(n, z - side * step, part if step == 3 else None)
            send(block, block, out_ring, in_ring + 4 * n + step, at(row, child, z + side, core))

    def ring_end(n):
        ring_wait(n, 3)
        for zz in range(8):
            k_hi[:, :, zz], k_lo[:, :, zz] = split(p_all[n, zz])
            if n % 2:
                even, odd = p_all[n - 1, zz], p_all[n, zz]
                for k, block in enumerate((merge(even, odd), merge_high(even, odd))):
                    hi, lo = split(block)
                    p_hi[2 * k:2 * k + 2, :, zz, :, 64 * n - 64:64 * n + 64] = hi
                    p_lo[2 * k:2 * k + 2, :, zz, :, 64 * n - 64:64 * n + 64] = lo

    y_up, y_down, y_far = lax.rem(row + 2, 8), lax.rem(row + 6, 8), lax.rem(row + 4, 8)
    x_far = row + 1 - 2 * lax.rem(row, 2)

    out_plane, in_plane = sems(0, 2), sems(1, 3 * NCHUNK)

    def plane_copy(u, k, r, to):
        send(x_all.at[u, r, core], x_all.at[u, r, core], out_plane, in_plane + 3 * u + k, (to, col))

    def plane_send(u):
        for to in (y_far, x_far, y_up, y_down):
            plane_copy(u, 0, row, to)

    def plane_pass(u):
        wait_recv(x_all.at[u, 0:4, 0], in_plane + 3 * u)
        plane_copy(u, 1, x_far, y_up)
        plane_copy(u, 1, x_far, y_down)
        plane_copy(u, 1, y_far, x_far)

    def plane_end(u):
        wait_recv(x_all.at[u, 0:3, 0], in_plane + 3 * u + 1)
        send(x_all.at[u, :, core], x_all.at[u, :, core], out_plane + 1, in_plane + 3 * u + 2, sib)

    def plane_wait(u):
        wait_recv(x_all.at[u, :, 0], in_plane + 3 * u + 2)

    out_mid, out_far, in_mid, in_far = sems(0), sems(0), sems(1, NCHUNK), sems(1, NCHUNK)
    out_cross, in_cross = sems(0, 3), sems(1, 3)
    out_g, in_g = sems(0, 2), sems(1, 2)
    out_s, in_s = sems(0, 3), sems(1, 3)

    def sel_send():
        select()
        for d in (4, 5, 3, 2, 6, 7, 1, 0):
            to = lax.rem(row + d, PLANE)
            if d:
                send(sel.at[child], s_all.at[row, core, child], out_s, in_s, (to, col))
            send(sel.at[1 - child], s_all.at[row, core, child], out_s + 1, in_s + 1, at(to, 1 - child, z, core))

    def sel_pass():
        wait_recv(s_all.at[0:7, 0, 0], in_s)
        wait_recv(s_all.at[:, 0, 0], in_s + 1)
        send(s_all.at[:, core], s_all.at[:, core], out_s + 2, in_s + 2, sib)

    def sel_end():
        wait_recv(s_all.at[:, 0], in_s + 2)

    def s_end():
        sel_pass()
        sel_end()
        pos = lax.broadcasted_iota(jnp.int32, (256, 256), 0)
        old = lax.broadcasted_iota(jnp.int32, (256, 256), 1)
        a, k, j, r, u = pos >> 6, (pos >> 5) & 1, (pos >> 4) & 1, (pos >> 1) & 7, pos & 1
        order = jnp.where(old == r * 32 + j * 16 + k * 8 + a * 2 + u, 1.0, 0.0).astype(BF16)
        hi, lo = split(s_all[...].reshape(256, 2048))
        s_cat[0:256] = mm(order, hi).astype(BF16)
        s_cat[256:512] = mm(order, lo).astype(BF16)

    def x_compute(n):
        b_hi, b_lo = k_hi[...].reshape(1024, 128), k_lo[...].reshape(1024, 128)
        parts = []
        for k in range(2):
            x = mm(s_cat[:, 1024 * k:1024 * k + 1024], b_hi)
            parts.append(x[0:256] + (x[256:512] + mm(s_cat[0:256, 1024 * k:1024 * k + 1024], b_lo)))
        x = -(parts[0] + pltpu.roll(parts[1], 64, 1))
        if n % 2:
            x_own[n // 2] = merge(x_own[n // 2].reshape(256, 128), x).reshape(4, 2, 32, 128)
        else:
            x_own[n // 2] = x.reshape(4, 2, 32, 128)
        x_send[n] = x.T[0:64]

        @pl.when(mid_self)
        def _():
            x_mid[n] = x_send[n]

        @pl.when(jnp.logical_not(mid_self))
        def _():
            send(x_send.at[n], x_mid.at[n], out_mid, in_mid + n, (mid_row, col))

    def cross_send(n):
        for k, d in enumerate(QUAD):
            c2, j2 = quad(d)
            send(x_own.at[n, :, c2, pl.ds(pl.multiple_of(16 * j2, 16), 16), :], c_in.at[child, core, n],
                 out_cross + k, in_cross + k, at(row, c2, z, j2))
        c_in[child, core, n] = x_own[n, :, child, pl.ds(pl.multiple_of(16 * core, 16), 16), :]

    def mid_pass(u):
        @pl.when(jnp.logical_not(mid_self))
        def _():
            wait_recv(x_mid.at[u], in_mid + u)

        @pl.when(far_self)
        def _():
            x_all[u, row, core] = x_mid[u]

        @pl.when(jnp.logical_not(far_self))
        def _():
            send(x_mid.at[u], x_all.at[u, row, half2], out_far, in_far + u, far)

    def far_pass(u):
        @pl.when(jnp.logical_not(far_self))
        def _():
            wait_recv(x_all.at[u, 0, 0], in_far + u)
        plane_send(u)

    def plane_slot(zz, h):
        w = bit_xor(h, zz % 2)
        ee = lax.rem(m - zz // 2 - 2 * h + 16, 4)
        return 4 * w + 2 * lax.div(ee, 2) + bit_xor(lax.rem(ee, 2), w)

    def g_compute(u):
        plane_wait(u)
        for rel in range(2):
            h = bit_xor(child, rel)
            for zz in range(8):
                x_hi, x_lo = split(x_all[u, plane_slot(zz, h), h])
                x_cat[64 * rel:64 * rel + 64, 256 * zz:256 * zz + 256] = x_hi
                x_cat[64 * rel + 128:64 * rel + 192, 256 * zz:256 * zz + 256] = x_lo
        b_hi = jnp.concatenate([p_hi[:, :, zz].reshape(256, 384) for zz in range(8)])
        g = mm(x_cat[...], b_hi)
        b_lo = jnp.concatenate([p_lo[:, :, zz].reshape(256, 384) for zz in range(8)])
        g = g[0:128] + (g[128:256] + mm(x_cat[0:128], b_lo))
        g_own[u] = g.reshape(2, 64, 384)

    def g_send(u):
        j2, k = u // 3, u % 3
        send(g_own.at[u, 1], g_in.at[child, core, k], out_g + 1, in_g + 1, at(row, 1 - child, z, j2))

        @pl.when(core == j2)
        def _():
            g_in[child, core, k] = g_own[u, 0]

        @pl.when(core != j2)
        def _():
            send(g_own.at[u, 0], g_in.at[child, core, k], out_g, in_g, sib)

    def cross_write():
        for k in range(3):
            wait_recv(c_in.at[0, 0], in_cross + k)
        for c in range(2):
            for h in range(2):
                for n in range(3):
                    cross[c, :, :, 384 * h + 128 * n:384 * h + 128 * n + 128] = c_in[c, h, n]

    def cov_write():
        loads[2].wait()
        wait_recv(g_in.at[0, 0], in_g)
        wait_recv(g_in.at[0], in_g + 1)
        for c in range(2):
            for h in range(2):
                cov[c, :, 384 * h:384 * h + 384] = inverse[c, :, 384 * h:384 * h + 384] - g_in[c, h].reshape(192, 384)

    quad_send(0)
    quad_send(1)
    quad_send(2)
    sel_send()
    quad_wait(0)
    ring(0, 0)
    ring(1, 0)
    quad_wait(1)
    ring(2, 0)
    ring(0, 1)
    ring(1, 1)
    ring(0, 2)
    ring(2, 1)
    ring(1, 2)
    ring(0, 3)
    quad_wait(2)
    ring(3, 0)
    ring(2, 2)
    ring(1, 3)
    ring(3, 1)
    ring(4, 0)
    s_end()
    ring_end(0)
    x_compute(0)
    ring(2, 3)
    ring(3, 2)
    ring_end(1)
    x_compute(1)
    ring(4, 1)
    ring(5, 0)
    mid_pass(0)
    mid_pass(1)
    ring(3, 3)
    ring(4, 2)
    ring_end(2)
    x_compute(2)
    cross_send(0)
    far_pass(0)
    ring(5, 1)
    ring(4, 3)
    mid_pass(2)
    far_pass(1)
    ring_end(3)
    x_compute(3)
    ring(5, 2)
    ring(5, 3)
    plane_pass(0)
    mid_pass(3)
    far_pass(2)
    cross_send(1)
    ring_end(4)
    x_compute(4)
    plane_pass(1)
    plane_end(0)
    mid_pass(4)
    far_pass(3)
    plane_pass(2)
    plane_end(1)
    ring_end(5)
    x_compute(5)
    far_pass(4)
    plane_pass(3)
    mid_pass(5)
    plane_end(2)
    g_compute(0)
    g_send(0)
    g_compute(1)
    g_send(1)
    plane_end(3)
    plane_pass(4)
    g_compute(2)
    g_send(2)
    far_pass(5)
    cross_send(2)
    g_compute(3)
    g_send(3)
    plane_end(4)
    plane_pass(5)
    g_compute(4)
    g_send(4)
    cross_write()
    plane_end(5)
    g_compute(5)
    g_send(5)
    cov_write()

    for k in range(3):
        wait_send(packed.at[0, 0], out_quad + k)
        wait_send(c_in.at[0, 0], out_cross + k)
    wait_send(s_all.at[0:7, 0, 0], out_s)
    wait_send(s_all.at[:, 0, 0], out_s + 1)
    wait_send(s_all.at[:, 0], out_s + 2)
    wait_send(p_all.at[:, 0:7], out_ring)
    wait_send(x_all.at[:, 0:7, 0], out_plane)
    wait_send(x_all.at[:, :, 0], out_plane + 1)
    wait_send(g_own.at[0:3, 0], out_g)
    wait_send(g_own.at[:, 0], out_g + 1)

    @pl.when(jnp.logical_not(mid_self))
    def _():
        wait_send(x_send, out_mid)

    @pl.when(jnp.logical_not(far_self))
    def _():
        wait_send(x_mid, out_far)


N_OUT, N_IN = 16, 65


def body(top_inverse, normed_panel, child_inverse, structure):
    vmem = pl.BlockSpec(memory_space=pltpu.VMEM)
    panel = normed_panel.reshape(2, 2, 2, 16, 768)
    return pl.pallas_call(
        kernel,
        out_shape=(jax.ShapeDtypeStruct((2, 4, 16, 768), F32), jax.ShapeDtypeStruct((2, 192, 768), F32)),
        in_specs=[pl.BlockSpec(memory_space=pltpu.SMEM)] + [pl.BlockSpec(memory_space=pl.ANY)] * 3,
        out_specs=(vmem, vmem),
        scratch_shapes=[
            pltpu.VMEM((24, 2, 24, 512), F32),
            pltpu.VMEM((2, 2, 2, 16, 768), F32),
            pltpu.VMEM((2, 2, 6, 2, 16, 128), F32),
            pltpu.VMEM((2, 192, 768), F32),
            pltpu.VMEM((2, 8, 2048), F32),
            pltpu.VMEM((8, 2, 2, 8, 2048), F32),
            pltpu.VMEM((512, 2048), BF16),
            pltpu.VMEM((NCHUNK, 8, 2, 2, 32, 128), F32),
            pltpu.VMEM((2, 2, 8, 32, 128), BF16),
            pltpu.VMEM((2, 2, 8, 32, 128), BF16),
            pltpu.VMEM((4, 2, 8, 32, 384), BF16),
            pltpu.VMEM((4, 2, 8, 32, 384), BF16),
            pltpu.VMEM((3, 4, 2, 32, 128), F32),
            pltpu.VMEM((NCHUNK, 64, 256), F32),
            pltpu.VMEM((NCHUNK, 64, 256), F32),
            pltpu.VMEM((NCHUNK, 8, 2, 64, 256), F32),
            pltpu.VMEM((256, 2048), BF16),
            pltpu.VMEM((NCHUNK, 2, 64, 384), F32),
            pltpu.VMEM((2, 2, 3, 64, 384), F32),
            pltpu.VMEM((2, 2, 3, 4, 16, 128), F32),
            pltpu.SemaphoreType.DMA((N_OUT,)),
            pltpu.SemaphoreType.DMA((N_IN,)),
            pltpu.SemaphoreType.DMA((3,)),
        ],
        compiler_params=pltpu.CompilerParams(collective_id=0, has_side_effects=True, vmem_limit_bytes=60 * 2**20),
        name="selected_inverse",
    )(structure, top_inverse, panel, child_inverse)


def solution(mesh):
    in_specs = (
        P(None, ("pcol", "prow"), None, None),
        P(None, None, "pcol", "prow"),
        P(None, "pcol", "prow"),
        P(),
    )
    out_specs = (P(None, None, "pcol", "prow"), P(None, "pcol", "prow"))
    return jax.shard_map(body, mesh=mesh, in_specs=in_specs, out_specs=out_specs, check_vma=False)
```

time: 442 us -> 102 us (0.23)
  waiting for transfers between devices: 391 us -> 0 us
  Pallas kernels: 0 us -> 97.3 us
  matrix products: 25.8 us -> 0 us
  between operations: 13.9 us -> 0.64 us
  other arithmetic: 7 us -> 0 us
    all_gather x3 -> x0, waiting for transfers between devices: 210 us -> none  [the longest x1 82 us: body(): cross_full = lax.all_gather(cross_cov, 'pcol', axis=2, tiled=True)]
    psum x1 -> x0, waiting for transfers between devices: 180 us -> none  [broadcast(): return lax.psum(kept, axis)]
    pallas_call x0 -> x1, Pallas kernels: none -> 97.3 us  [body(): pl.pallas_call(kernel, out_shape=(jax.ShapeDtypeStruct((2, 4, 16, 768), F...]
    dot_general x2 -> x0, matrix products: 25.8 us -> none  [the longest x1 13.5 us: body(): jnp.einsum('cbvj,cbvk->cjk', column_panel, cross_full, precision=lax.Prec...]
    select_n x2 -> x0, other arithmetic: 6.03 us -> none  [the longest x1 5.87 us: broadcast(): jnp.where(lax.axis_index(axis) == source, value, 0).astype(value.dtype)]
  transfers between devices with their start and end apart: 4 -> 0, of which waited for: 4 -> 0; matrix products, arithmetic and copies ran while one was open for 5% -> 0% of each run, Pallas kernels for 0% -> 0%
where the time goes in v2:
time: 102 us
  Pallas kernels  97.3 us (95%)
  local copies, waits for them, and re-layouts  4.13 us (4%)
    pallas_call x1, Pallas kernels, body(): pl.pallas_call(kernel, out_shape=(jax.ShapeDtypeStruct((2, 4, 16, 768), F...  97.3 us
    unnamed x2, local copies, waits for them, and re-layouts  4.13 us

profile of v2, /device:TPU:1, one launch (start us, length us, event | category | flops | bytes accessed | tf_op | source)
XLA Modules:
  0.0 102.1 jit_solution(10391456528632721421)
XLA Ops:
  0.6 97.3 %selected_inverse.1 = (f32[2,4,16,768]{3,2,1,0:T(8,128)}, f32[2,192,768]{2,1,0:T(8,128)}) custom-call(s32[2,4]{1,0:T(2,128)} %structure.1, f32[24,2,24,512]{3,2,1,0:T(8,128)} %top_hbm.1, f32[2,2,2,16,768]{4,3,2,1,0:T(8,128)} %bitcast.1, f32[2,192,768]{2,1,0:T(8,128)} %inverse_hbm.1), custom_call_target="tpu_custom_call" | custom-call | tf_op jit(solution)/shard_map/selected_inverse/pallas_call | solution.py:432
  97.9 1.8 %copy.8 = f32[2,4,16,768]{3,2,1,0:T(8,128)} copy(f32[2,4,16,768]{3,2,1,0:T(8,128)} %get-tuple-element.4) | data formatting | bytes 786432
  99.7 2.4 %copy.9 = f32[2,192,768]{2,1,0:T(8,128)} copy(f32[2,192,768]{2,1,0:T(8,128)} %get-tuple-element.5) | data formatting | bytes 2359296

commit v3 on v2

--- a/solution.py
+++ b/solution.py
@@ -158,12 +158,14 @@
         ring_wait(n, 3)
         for zz in range(8):
             k_hi[:, :, zz], k_lo[:, :, zz] = split(p_all[n, zz])
-            if n % 2:
-                even, odd = p_all[n - 1, zz], p_all[n, zz]
-                for k, block in enumerate((merge(even, odd), merge_high(even, odd))):
-                    hi, lo = split(block)
-                    p_hi[2 * k:2 * k + 2, :, zz, :, 64 * n - 64:64 * n + 64] = hi
-                    p_lo[2 * k:2 * k + 2, :, zz, :, 64 * n - 64:64 * n + 64] = lo
+
+    def unpack(n):
+        for zz in range(8):
+            even, odd = p_all[2 * n, zz], p_all[2 * n + 1, zz]
+            for k, block in enumerate((merge(even, odd), merge_high(even, odd))):
+                hi, lo = split(block)
+                p_hi[2 * k:2 * k + 2, :, zz, :, 128 * n:128 * n + 128] = hi
+                p_lo[2 * k:2 * k + 2, :, zz, :, 128 * n:128 * n + 128] = lo
 
     y_up, y_down, y_far = lax.rem(row + 2, 8), lax.rem(row + 6, 8), lax.rem(row + 4, 8)
     x_far = row + 1 - 2 * lax.rem(row, 2)
@@ -181,7 +183,10 @@
         wait_recv(x_all.at[u, 0:4, 0], in_plane + 3 * u)
         plane_copy(u, 1, x_far, y_up)
         plane_copy(u, 1, x_far, y_down)
-        plane_copy(u, 1, y_far, x_far)
+        if u < 3:
+            plane_copy(u, 1, y_far, x_far)
+        else:
+            plane_copy(u, 1, x_far, y_far)
 
     def plane_end(u):
         wait_recv(x_all.at[u, 0:3, 0], in_plane + 3 * u + 1)
@@ -347,59 +352,62 @@
     ring(4, 1)
     ring(5, 0)
     mid_pass(0)
-    mid_pass(1)
     ring(3, 3)
     ring(4, 2)
+    mid_pass(1)
     ring_end(2)
     x_compute(2)
-    cross_send(0)
-    far_pass(0)
     ring(5, 1)
     ring(4, 3)
+    far_pass(0)
+    ring_end(3)
+    x_compute(3)
+    cross_send(0)
+    unpack(0)
+    ring(5, 2)
     mid_pass(2)
     far_pass(1)
-    ring_end(3)
-    x_compute(3)
-    ring(5, 2)
     ring(5, 3)
     plane_pass(0)
+    ring_end(4)
+    x_compute(4)
     mid_pass(3)
     far_pass(2)
-    cross_send(1)
-    ring_end(4)
-    x_compute(4)
     plane_pass(1)
+    ring_end(5)
+    x_compute(5)
+    mid_pass(4)
+    mid_pass(5)
     plane_end(0)
-    mid_pass(4)
     far_pass(3)
     plane_pass(2)
     plane_end(1)
-    ring_end(5)
-    x_compute(5)
     far_pass(4)
     plane_pass(3)
-    mid_pass(5)
+    far_pass(5)
     plane_end(2)
+    cross_send(1)
+    unpack(1)
+    unpack(2)
     g_compute(0)
     g_send(0)
+    plane_pass(4)
+    plane_end(3)
     g_compute(1)
     g_send(1)
-    plane_end(3)
-    plane_pass(4)
+    plane_pass(5)
     g_compute(2)
     g_send(2)
-    far_pass(5)
-    cross_send(2)
+    plane_end(4)
     g_compute(3)
     g_send(3)
-    plane_end(4)
-    plane_pass(5)
+    cross_send(2)
     g_compute(4)
     g_send(4)
-    cross_write()
     plane_end(5)
     g_compute(5)
     g_send(5)
+    cross_write()
     cov_write()
 
     for k in range(3):
@@ -459,7 +467,7 @@
             pltpu.SemaphoreType.DMA((N_IN,)),
             pltpu.SemaphoreType.DMA((3,)),
         ],
-        compiler_params=pltpu.CompilerParams(collective_id=0, has_side_effects=True, vmem_limit_bytes=60 * 2**20),
+        compiler_params=pltpu.CompilerParams(collective_id=0, has_side_effects=True, vmem_limit_bytes=52 * 2**20),
         name="selected_inverse",
     )(structure, top_inverse, panel, child_inverse)
 

time: 102 us -> 97.8 us (0.959)
  Pallas kernels: 97.3 us -> 93.6 us
    pallas_call x1, Pallas kernels: 97.3 us -> 93.6 us  [body(): pl.pallas_call(kernel, out_shape=(jax.ShapeDtypeStruct((2, 4, 16, 768), F...]
    unnamed x2 -> x6, local copies, waits for them, and re-layouts: 4.13 us -> 3.43 us
where the time goes in v3:
time: 97.8 us; the launch traced here: 97.7 us
  Pallas kernels  93.6 us (96%)
  local copies, waits for them, and re-layouts  3.43 us (4%)
    pallas_call x1, Pallas kernels, body(): pl.pallas_call(kernel, out_shape=(jax.ShapeDtypeStruct((2, 4, 16, 768), F...  93.6 us
    unnamed x6, local copies, waits for them, and re-layouts  3.43 us

profile of v3, /device:TPU:1, one launch (start us, length us, event | category | flops | bytes accessed | tf_op | source)
XLA Modules:
  0.0 97.7 jit_solution(9367333120016948866)
XLA Ops:
  0.6 0.0 copy-start
  0.6 1.0 %copy-done = f32[2,4,16,768]{3,2,1,0:T(8,128)S(1)} copy-done((f32[2,4,16,768]{3,2,1,0:T(8,128)S(1)}, f32[2,4,16,768]{3,2,1,0:T(8,128)}, u32[]{:S(2)}) %copy-start) | copy-done | bytes 393240
  1.6 0.0 copy-start.1
  1.6 0.7 copy-done.1
  2.3 93.6 %selected_inverse.1 = (f32[2,4,16,768]{3,2,1,0:T(8,128)S(1)}, f32[2,192,768]{2,1,0:T(8,128)S(1)}) custom-call(s32[2,4]{1,0:T(2,128)S(1)} %copy-done.1, f32[24,2,24,512]{3,2,1,0:T(8,128)} %top_hbm.1, f32[2,2,2,16,768]{4,3,2,1,0:T(8,128)S(1)} %bitcast.1, f32[2,192,768]{2,1,0:T(8,128)} %inverse_hbm.1), custom_call_target="tpu_custom_call" | custom-call | tf_op jit(solution)/shard_map/selected_inverse/pallas_call | solution.py:440
  95.9 0.7 copy.8
  96.7 1.0 %copy.9 = f32[2,192,768]{2,1,0:T(8,128)} copy(f32[2,192,768]{2,1,0:T(8,128)S(1)} %get-tuple-element.5) | data formatting | bytes 2359296
Async XLA Ops:
  0.6 1.0 %copy-start = (f32[2,4,16,768]{3,2,1,0:T(8,128)S(1)}, f32[2,4,16,768]{3,2,1,0:T(8,128)}, u32[]{:S(2)}) copy-start(f32[2,4,16,768]{3,2,1,0:T(8,128)} %param.5) | copy-start | bytes 1179652
  1.6 0.7 copy-start.1

commit v4 on v3

--- a/solution.py
+++ b/solution.py
@@ -98,7 +98,6 @@
     greet(at(row, child, z - 1, core))
     for d in range(1, PLANE):
         greet((lax.rem(row + d, PLANE), col))
-        greet(at(lax.rem(row + d, PLANE), 1 - child, z, core))
 
     @pl.when(jnp.logical_not(far_self))
     def _():
@@ -116,19 +115,6 @@
                     packed[c, j, 2 * n + 1, b] = merge_high(low, high)
     for t in range(NCHUNK):
         p_all[t, z, :, child, pl.ds(pl.multiple_of(16 * core, 16), 16), :] = packed[child, core, t]
-    pl.semaphore_wait(barrier, 19 + 2 * (1 - far_self.astype(jnp.int32)))
-
-    out_quad, in_quad = sems(0, 3), sems(1, 3)
-
-    def quad_send(n):
-        for k, d in enumerate(QUAD):
-            c2, j2 = quad(d)
-            send(packed.at[c2, j2, 2 * n:2 * n + 2], p_all.at[2 * n:2 * n + 2, z, :, child, pl.ds(pl.multiple_of(16 * core, 16), 16), :],
-                 out_quad + k, in_quad + n, at(row, c2, z, j2))
-
-    def quad_wait(n):
-        wait_recv(packed.at[0, 0], in_quad + n)
-
     def select():
         loads[1].wait()
         for c in range(2):
@@ -138,6 +124,20 @@
                         sel[c, 2 * a + u:2 * a + u + 1, 512 * b:512 * b + 512] = top[structure[c, a], u, pl.ds(structure[c, b], 1), :]
         s_all[row, core, child] = sel[child]
 
+    select()
+    pl.semaphore_wait(barrier, 12 + 2 * (1 - far_self.astype(jnp.int32)))
+
+    out_quad, in_quad = sems(0, 3), sems(1, 3)
+
+    def quad_send(n):
+        for k, d in enumerate(QUAD):
+            c2, j2 = quad(d)
+            send(packed.at[c2, j2, 2 * n:2 * n + 2], p_all.at[2 * n:2 * n + 2, z, :, child, pl.ds(pl.multiple_of(16 * core, 16), 16), :],
+                 out_quad + k, in_quad + n, at(row, c2, z, j2))
+
+    def quad_wait(n):
+        wait_recv(packed.at[0, 0], in_quad + n)
+
     out_ring, in_ring = sems(0), sems(1, 4 * NCHUNK)
 
     def chunk(n, zz, part=None):
@@ -183,10 +183,7 @@
         wait_recv(x_all.at[u, 0:4, 0], in_plane + 3 * u)
         plane_copy(u, 1, x_far, y_up)
         plane_copy(u, 1, x_far, y_down)
-        if u < 3:
-            plane_copy(u, 1, y_far, x_far)
-        else:
-            plane_copy(u, 1, x_far, y_far)
+        plane_copy(u, 1, y_far, x_far)
 
     def plane_end(u):
         wait_recv(x_all.at[u, 0:3, 0], in_plane + 3 * u + 1)
@@ -198,26 +195,34 @@
     out_mid, out_far, in_mid, in_far = sems(0), sems(0), sems(1, NCHUNK), sems(1, NCHUNK)
     out_cross, in_cross = sems(0, 3), sems(1, 3)
     out_g, in_g = sems(0, 2), sems(1, 2)
-    out_s, in_s = sems(0, 3), sems(1, 3)
+    out_s, in_s = sems(0, 3), sems(1, 4)
+
+    def sel_copy(k, r, to):
+        send(s_all.at[r, core], s_all.at[r, core], out_s + 1, in_s + k, (to, col))
 
     def sel_send():
-        select()
-        for d in (4, 5, 3, 2, 6, 7, 1, 0):
-            to = lax.rem(row + d, PLANE)
-            if d:
-                send(sel.at[child], s_all.at[row, core, child], out_s, in_s, (to, col))
-            send(sel.at[1 - child], s_all.at[row, core, child], out_s + 1, in_s + 1, at(to, 1 - child, z, core))
+        send(sel.at[1 - child], s_all.at[row, core, child], out_s, in_s, at(row, 1 - child, z, core))
+
+    def sel_spread():
+        wait_recv(s_all.at[0, 0, 0], in_s)
+        for to in (y_far, x_far, y_up, y_down):
+            sel_copy(1, row, to)
 
     def sel_pass():
-        wait_recv(s_all.at[0:7, 0, 0], in_s)
-        wait_recv(s_all.at[:, 0, 0], in_s + 1)
-        send(s_all.at[:, core], s_all.at[:, core], out_s + 2, in_s + 2, sib)
+        wait_recv(s_all.at[0:4, 0], in_s + 1)
+        sel_copy(2, x_far, y_up)
+        sel_copy(2, x_far, y_down)
+        sel_copy(2, y_far, x_far)
+
+    def sel_join():
+        wait_recv(s_all.at[0:3, 0], in_s + 2)
+        send(s_all.at[:, core], s_all.at[:, core], out_s + 2, in_s + 3, sib)
 
     def sel_end():
-        wait_recv(s_all.at[:, 0], in_s + 2)
+        wait_recv(s_all.at[:, 0], in_s + 3)
 
     def s_end():
-        sel_pass()
+        sel_join()
         sel_end()
         pos = lax.broadcasted_iota(jnp.int32, (256, 256), 0)
         old = lax.broadcasted_iota(jnp.int32, (256, 256), 1)
@@ -322,12 +327,13 @@
                 cov[c, :, 384 * h:384 * h + 384] = inverse[c, :, 384 * h:384 * h + 384] - g_in[c, h].reshape(192, 384)
 
     quad_send(0)
+    sel_send()
     quad_send(1)
     quad_send(2)
-    sel_send()
     quad_wait(0)
     ring(0, 0)
     ring(1, 0)
+    sel_spread()
     quad_wait(1)
     ring(2, 0)
     ring(0, 1)
@@ -335,6 +341,7 @@
     ring(0, 2)
     ring(2, 1)
     ring(1, 2)
+    sel_pass()
     ring(0, 3)
     quad_wait(2)
     ring(3, 0)
@@ -413,8 +420,8 @@
     for k in range(3):
         wait_send(packed.at[0, 0], out_quad + k)
         wait_send(c_in.at[0, 0], out_cross + k)
-    wait_send(s_all.at[0:7, 0, 0], out_s)
-    wait_send(s_all.at[:, 0, 0], out_s + 1)
+    wait_send(s_all.at[0, 0, 0], out_s)
+    wait_send(s_all.at[0:7, 0], out_s + 1)
     wait_send(s_all.at[:, 0], out_s + 2)
     wait_send(p_all.at[:, 0:7], out_ring)
     wait_send(x_all.at[:, 0:7, 0], out_plane)
@@ -431,7 +438,7 @@
         wait_send(x_mid, out_far)
 
 
-N_OUT, N_IN = 16, 65
+N_OUT, N_IN = 16, 66
 
 
 def body(top_inverse, normed_panel, child_inverse, structure):

time: 97.8 us -> 98.5 us (level)
  no operation moved by 1% of the time
where the time goes in v4:
time: 98.5 us; the launch traced here: 98.3 us
  Pallas kernels  94.2 us (96%)
  local copies, waits for them, and re-layouts  3.43 us (3%)
    pallas_call x1, Pallas kernels, body(): pl.pallas_call(kernel, out_shape=(jax.ShapeDtypeStruct((2, 4, 16, 768), F...  94.2 us
    unnamed x6, local copies, waits for them, and re-layouts  3.43 us

profile of v4, /device:TPU:1, one launch (start us, length us, event | category | flops | bytes accessed | tf_op | source)
XLA Modules:
  0.0 98.3 jit_solution(13905093077923525731)
XLA Ops:
  0.6 0.0 copy-start
  0.6 1.0 %copy-done = f32[2,4,16,768]{3,2,1,0:T(8,128)S(1)} copy-done((f32[2,4,16,768]{3,2,1,0:T(8,128)S(1)}, f32[2,4,16,768]{3,2,1,0:T(8,128)}, u32[]{:S(2)}) %copy-start) | copy-done | bytes 393240
  1.6 0.0 copy-start.1
  1.6 0.7 copy-done.1
  2.3 94.2 %selected_inverse.1 = (f32[2,4,16,768]{3,2,1,0:T(8,128)S(1)}, f32[2,192,768]{2,1,0:T(8,128)S(1)}) custom-call(s32[2,4]{1,0:T(2,128)S(1)} %copy-done.1, f32[24,2,24,512]{3,2,1,0:T(8,128)} %top_hbm.1, f32[2,2,2,16,768]{4,3,2,1,0:T(8,128)S(1)} %bitcast.1, f32[2,192,768]{2,1,0:T(8,128)} %inverse_hbm.1), custom_call_target="tpu_custom_call" | custom-call | tf_op jit(solution)/shard_map/selected_inverse/pallas_call | solution.py:447
  96.6 0.7 copy.8
  97.3 1.0 %copy.9 = f32[2,192,768]{2,1,0:T(8,128)} copy(f32[2,192,768]{2,1,0:T(8,128)S(1)} %get-tuple-element.5) | data formatting | bytes 2359296
Async XLA Ops:
  0.6 1.0 %copy-start = (f32[2,4,16,768]{3,2,1,0:T(8,128)S(1)}, f32[2,4,16,768]{3,2,1,0:T(8,128)}, u32[]{:S(2)}) copy-start(f32[2,4,16,768]{3,2,1,0:T(8,128)} %param.5) | copy-start | bytes 1179652
  1.6 0.7 copy-start.1

commit v5 on v4

--- a/solution.py
+++ b/solution.py
@@ -37,7 +37,7 @@
     return jnp.dot(a, b, preferred_element_type=F32)
 
 
-def kernel(structure, top_hbm, panel_hbm, inverse_hbm, cross, cov, top, panel, packed, inverse, sel, s_all, s_cat, p_all, k_hi, k_lo, p_hi, p_lo,
+def kernel(structure, top_hbm, panel_hbm, inverse_hbm, cross, cov, top, panel, packed, inverse, sel, s_all, s_cat, p_all, k_all, p_split,
            x_own, x_send, x_mid, x_all, x_cat, g_own, g_in, c_in, ss, rs, ls):
     row, col = lax.axis_index("prow"), lax.axis_index("pcol")
     child, z, core = lax.div(col, 16), lax.rem(lax.div(col, 2), 8), lax.rem(col, 2)
@@ -157,15 +157,15 @@
     def ring_end(n):
         ring_wait(n, 3)
         for zz in range(8):
-            k_hi[:, :, zz], k_lo[:, :, zz] = split(p_all[n, zz])
+            k_all[:, :, zz, :, 0:128], k_all[:, :, zz, :, 128:256] = split(p_all[n, zz])
 
     def unpack(n):
         for zz in range(8):
             even, odd = p_all[2 * n, zz], p_all[2 * n + 1, zz]
             for k, block in enumerate((merge(even, odd), merge_high(even, odd))):
                 hi, lo = split(block)
-                p_hi[2 * k:2 * k + 2, :, zz, :, 128 * n:128 * n + 128] = hi
-                p_lo[2 * k:2 * k + 2, :, zz, :, 128 * n:128 * n + 128] = lo
+                p_split[2 * k:2 * k + 2, :, zz, :, 128 * n:128 * n + 128] = hi
+                p_split[2 * k:2 * k + 2, :, zz, :, 384 + 128 * n:512 + 128 * n] = lo
 
     y_up, y_down, y_far = lax.rem(row + 2, 8), lax.rem(row + 6, 8), lax.rem(row + 4, 8)
     x_far = row + 1 - 2 * lax.rem(row, 2)
@@ -233,11 +233,11 @@
         s_cat[256:512] = mm(order, lo).astype(BF16)
 
     def x_compute(n):
-        b_hi, b_lo = k_hi[...].reshape(1024, 128), k_lo[...].reshape(1024, 128)
+        b = k_all[...].reshape(1024, 256)
         parts = []
         for k in range(2):
-            x = mm(s_cat[:, 1024 * k:1024 * k + 1024], b_hi)
-            parts.append(x[0:256] + (x[256:512] + mm(s_cat[0:256, 1024 * k:1024 * k + 1024], b_lo)))
+            x = mm(s_cat[:, 1024 * k:1024 * k + 1024], b)
+            parts.append(x[0:256, 0:128] + (x[256:512, 0:128] + x[0:256, 128:256]))
         x = -(parts[0] + pltpu.roll(parts[1], 64, 1))
         if n % 2:
             x_own[n // 2] = merge(x_own[n // 2].reshape(256, 128), x).reshape(4, 2, 32, 128)
@@ -292,10 +292,8 @@
                 x_hi, x_lo = split(x_all[u, plane_slot(zz, h), h])
                 x_cat[64 * rel:64 * rel + 64, 256 * zz:256 * zz + 256] = x_hi
                 x_cat[64 * rel + 128:64 * rel + 192, 256 * zz:256 * zz + 256] = x_lo
-        b_hi = jnp.concatenate([p_hi[:, :, zz].reshape(256, 384) for zz in range(8)])
-        g = mm(x_cat[...], b_hi)
-        b_lo = jnp.concatenate([p_lo[:, :, zz].reshape(256, 384) for zz in range(8)])
-        g = g[0:128] + (g[128:256] + mm(x_cat[0:128], b_lo))
+        g = mm(x_cat[...], jnp.concatenate([p_split[:, :, zz].reshape(256, 768) for zz in range(8)]))
+        g = g[0:128, 0:384] + (g[128:256, 0:384] + g[0:128, 384:768])
         g_own[u] = g.reshape(2, 64, 384)
 
     def g_send(u):
@@ -458,10 +456,8 @@
             pltpu.VMEM((8, 2, 2, 8, 2048), F32),
             pltpu.VMEM((512, 2048), BF16),
             pltpu.VMEM((NCHUNK, 8, 2, 2, 32, 128), F32),
-            pltpu.VMEM((2, 2, 8, 32, 128), BF16),
-            pltpu.VMEM((2, 2, 8, 32, 128), BF16),
-            pltpu.VMEM((4, 2, 8, 32, 384), BF16),
-            pltpu.VMEM((4, 2, 8, 32, 384), BF16),
+            pltpu.VMEM((2, 2, 8, 32, 256), BF16),
+            pltpu.VMEM((4, 2, 8, 32, 768), BF16),
             pltpu.VMEM((3, 4, 2, 32, 128), F32),
             pltpu.VMEM((NCHUNK, 64, 256), F32),
             pltpu.VMEM((NCHUNK, 64, 256), F32),

time: 98.5 us -> 98.3 us (level)
  no operation moved by 1% of the time
where the time goes in v5:
time: 98.3 us; the launch traced here: 98.1 us
  Pallas kernels  94.1 us (96%)
  local copies, waits for them, and re-layouts  3.43 us (3%)
    pallas_call x1, Pallas kernels, body(): pl.pallas_call(kernel, out_shape=(jax.ShapeDtypeStruct((2, 4, 16, 768), F...  94.1 us
    unnamed x6, local copies, waits for them, and re-layouts  3.43 us

profile of v5, /device:TPU:1, one launch (start us, length us, event | category | flops | bytes accessed | tf_op | source)
XLA Modules:
  0.0 98.1 jit_solution(4518993013695885542)
XLA Ops:
  0.6 0.0 copy-start
  0.6 1.0 %copy-done = f32[2,4,16,768]{3,2,1,0:T(8,128)S(1)} copy-done((f32[2,4,16,768]{3,2,1,0:T(8,128)S(1)}, f32[2,4,16,768]{3,2,1,0:T(8,128)}, u32[]{:S(2)}) %copy-start) | copy-done | bytes 393240
  1.6 0.0 copy-start.1
  1.6 0.7 copy-done.1
  2.3 94.1 %selected_inverse.1 = (f32[2,4,16,768]{3,2,1,0:T(8,128)S(1)}, f32[2,192,768]{2,1,0:T(8,128)S(1)}) custom-call(s32[2,4]{1,0:T(2,128)S(1)} %copy-done.1, f32[24,2,24,512]{3,2,1,0:T(8,128)} %top_hbm.1, f32[2,2,2,16,768]{4,3,2,1,0:T(8,128)S(1)} %bitcast.1, f32[2,192,768]{2,1,0:T(8,128)} %inverse_hbm.1), custom_call_target="tpu_custom_call" | custom-call | tf_op jit(solution)/shard_map/selected_inverse/pallas_call | solution.py:445
  96.4 0.7 copy.8
  97.1 1.0 %copy.9 = f32[2,192,768]{2,1,0:T(8,128)} copy(f32[2,192,768]{2,1,0:T(8,128)S(1)} %get-tuple-element.5) | data formatting | bytes 2359296
Async XLA Ops:
  0.6 1.0 %copy-start = (f32[2,4,16,768]{3,2,1,0:T(8,128)S(1)}, f32[2,4,16,768]{3,2,1,0:T(8,128)}, u32[]{:S(2)}) copy-start(f32[2,4,16,768]{3,2,1,0:T(8,128)} %param.5) | copy-start | bytes 1179652
  1.6 0.7 copy-start.1
